TPU v7x, 32 devices: a whole 2x2x4 slice. The times are simulated.
32 devices in a mesh: groups: 2 (over x), row: 16 (over z, y, core).
Axes of the slice: x: 2, y: 2, z: 4, core: 2. Of those that a mesh axis runs over, the one named last changes fastest.
Arguments:
- basis: float32 [8192, 128], P(('groups', 'row')), parts along dimension 0, may hold values from -6 to 6
- springs: float32 [8192], P(('groups', 'row')), parts along dimension 0, may hold values from 0.25 to 8
- tangent_blocks: float32 [4096, 4096], P(('groups', 'row')), parts along dimension 0, may hold values from -0.375 to 0.375
- tile_rows: int32 [4096], P(('groups', 'row')), parts along dimension 0, may hold values from 0 to 3
- tile_owner: int32 [4096, 1], P(('groups', 'row')), parts along dimension 0, may hold values from 0 to 15, as said below
- tile_offset: int32 [4096], P(('groups', 'row')), parts along dimension 0, may hold values from 0 to 3
- tile_count: int32 [32], P(('groups', 'row')), parts along dimension 0, may hold values from 32 to 128, as said below
Outputs:
- stiff_image: float32 [8192, 128], P(('groups', 'row')), parts along dimension 0
- reduced: float32 [256, 128], P('groups'), parts along dimension 0
There are 2 independent parts, one for each index of `groups`. A program takes and returns all parts, laid end to end along the dimension named above; each array names one. Nothing has to cross between parts.
Inputs may be any that keep to these rules, and one draw needn't show every extreme that they name: The first tile_count[d] slots of device d are live; some device has exactly 128. `tile_owner`: the slab is closed into a shell: every slot of device d names owner (d + o) mod 16 with o one of 0, 1, -1, 4, -4, 5, -5, 8. Among the slots of one device no owner appears more than 32 times, and owner d itself appears exactly 32 times in every device.
All inputs are finite; a program needn't handle non-finite values.
Results may differ from a plain program's by a relative error of at most 0.0003.
Values sent between devices are 32-bit elements; how exact they have to be, the bound alone decides.
No kernel may reach another device: no remote copies, remote signals or barrier semaphores. Data moves between devices by JAX's collectives and lax.ppermute only.
A program may use at most 128 MiB of HBM per device.

v0:
```python
import jax
import jax.numpy as jnp
from jax import lax
from jax.sharding import PartitionSpec as P

B = 64
MODES = 128
BR_DEV = 4
CAP = 128


def shards(basis, springs, tangent_blocks, tile_rows, tile_owner, tile_offset, tile_count):
    row_devices = lax.axis_size("row")
    dof_total = basis.shape[0] * row_devices
    own_blocks = basis.reshape(BR_DEV, B, MODES)
    square_blocks = tangent_blocks.reshape(CAP, B, B)
    owner_ids = tile_owner[:, 0]
    gathered = lax.all_gather(own_blocks, "row", axis=0, tiled=True)
    picked = gathered[owner_ids * BR_DEV + tile_offset]
    live_slot = (jnp.arange(CAP, dtype=jnp.int32) < tile_count[0]).astype(jnp.float32)
    row_ids = jnp.arange(BR_DEV, dtype=jnp.int32)
    products = jnp.einsum("sij,sjk->sik", square_blocks, picked, precision=lax.Precision.HIGHEST)
    row_select = (tile_rows[None, :] == row_ids[:, None]).astype(jnp.float32) * live_slot[None, :]
    summed = jnp.dot(row_select, products.reshape(CAP, B * MODES), precision=lax.Precision.HIGHEST)
    stiff_image = springs[:, None] * basis + summed.reshape(BR_DEV * B, MODES)
    partial_term = (
        jnp.einsum("rm,rn->mn", basis, stiff_image, precision=lax.Precision.HIGHEST) / dof_total
    )
    reduced = lax.psum(partial_term, "row")
    return (stiff_image, reduced)


def solution(mesh):
    in_specs = (
        P(("groups", "row"), None),
        P(("groups", "row")),
        P(("groups", "row"), None),
        P(("groups", "row")),
        P(("groups", "row"), None),
        P(("groups", "row")),
        P(("groups", "row")),
    )
    out_specs = (P(("groups", "row"), None), P("groups", None))
    return jax.shard_map(shards, mesh=mesh, in_specs=in_specs, out_specs=out_specs, check_vma=False)
```

profile of v0, /device:TPU:0, one launch (start us, length us, event | category | flops | bytes accessed | tf_op | source)
XLA Modules:
  0.0 162.7 jit_solution(6896301566178183216)
XLA Ops:
  7.2 0.0 all-gather.2.cloned.1.call-start
  7.2 0.7 all-gather.2.cloned.1.call-update
  7.9 0.0 all-reduce.2.cloned.1.call-start
  7.9 1.9 %copy.13 = f32[128,4096]{0,1:T(8,128)S(1)} copy(f32[128,4096]{1,0:T(8,128)} %param.9) | data formatting | bytes 4194304 | tf_op args[2]
  9.9 0.0 copy-start.4
  9.9 0.0 copy-start.5
  9.9 4.5 %copy.14 = f32[128,64,64]{2,1,0:T(8,128)} copy(f32[128,64,64]{0,2,1:T(8,128)S(1)} %bitcast.20) | data formatting | bytes 4194304 | tf_op jit(solution)/shard_map/reshape | solution.py:16
  15.1 0.0 copy-done.4
  15.1 0.0 copy-done.5
  15.1 39.2 %all-gather.2.cloned.1.call-done = f32[64,64,128]{2,1,0:T(8,128)} async-done(((f32[4,64,128]{2,1,0:T(8,128)}), f32[64,64,128]{2,1,0:T(8,128)}) %all-gather.2.cloned.1.call-update) | async-done | bytes 2097168 | tf_op jit(solution)/shard_map/all_gather | solution.py:18
  54.3 4.4 %gather_fusion = f32[128,64,128]{2,1,0:T(8,128)} fusion(f32[64,64,128]{2,1,0:T(8,128)} %all-gather.2.cloned.1.call-done, s32[1024]{0:T(1024)S(1)} %pad_clamp_fusion), kind=kCustom, calls=%fused_computation | custom fusion | bytes 8389120 | tf_op jit(solution)/shard_map/gather | solution.py:19
  58.6 0.0 copy-start.3
  58.6 6.5 %fusion.9 = f32[128,128,64]{1,2,0:T(8,128)S(1)} fusion(f32[128,64,128]{2,1,0:T(8,128)} %gather_fusion, f32[128,64,64]{2,1,0:T(8,128)} %copy.14), kind=kOutput, calls=%fused_computation.17 | convolution fusion | flops 805306368 | bytes 10485760 | tf_op jit(solution)/shard_map/sij,sjk->sik/dot_general | solution.py:22
  65.2 0.0 copy-start
  65.2 0.0 copy-start.2
  65.2 0.0 copy-done.3
  65.2 4.3 %fusion = f32[4,8192]{1,0:T(4,128)S(1)} fusion(f32[16,8,64,128]{3,2,1,0:T(8,128)S(1)} %bitcast.19, f32[128]{0:T(128)S(1)} %compare_convert_fusion, s32[128]{0:T(128)S(1)} %copy-done.3), kind=kOutput, calls=%fused_computation.1 | convolution fusion | flops 50332672 | bytes 4326400 | tf_op jit(solution)/shard_map/dot_general | solution.py:24
  69.6 0.1 reshape.28
  69.7 0.0 copy-done
  69.7 0.0 copy-done.2
  69.7 0.1 multiply_add_fusion
  69.8 0.0 copy-start.1
  69.8 1.0 fusion.3
  70.8 0.0 all-reduce.2.cloned.1.call-update
  70.8 83.4 %all-reduce.2.cloned.1.call-done = f32[128,128]{0,1:T(8,128)} async-done(((f32[128,128]{0,1:T(8,128)}), f32[128,128]{0,1:T(8,128)}) %all-reduce.2.cloned.1.call-update) | async-done | bytes 65552 | tf_op jit(solution)/shard_map/psum | solution.py:29
  154.2 1.6 copy.15
  155.8 0.0 copy-done.1
  (3 shorter events, 0.0 us)
Async XLA Ops:
  7.2 47.1 %all-gather.2.cloned.1.call-start = ((), (), s32[]{:S(2)}) async-start(), calls=%async_computation | async-start | bytes 2228224 | tf_op jit(solution)/shard_map/all_gather | solution.py:18
  7.9 146.3 %all-reduce.2.cloned.1.call-start = ((), (), s32[]{:S(2)}) async-start(), calls=%async_computation.1 | async-start | bytes 131072 | tf_op jit(solution)/shard_map/psum | solution.py:29
  9.9 5.2 %copy-start.4 = (s32[128]{0:T(128)S(1)}, s32[128]{0:T(128)}, u32[]{:S(2)}) copy-start(s32[128]{0:T(128)} %param.12) | copy-start | bytes 1540
  9.9 5.2 %copy-start.5 = (s32[128,1]{0,1:T(1,128)S(1)}, s32[128,1]{0,1:T(1,128)}, u32[]{:S(2)}) copy-start(s32[128,1]{0,1:T(1,128)} %param.11) | copy-start | bytes 1540
  58.6 6.6 %copy-start.3 = (s32[128]{0:T(128)S(1)}, s32[128]{0:T(128)}, u32[]{:S(2)}) copy-start(s32[128]{0:T(128)} %param.10) | copy-start | bytes 1540
  65.2 4.5 %copy-start = (f32[256,128]{1,0:T(8,128)S(1)}, f32[256,128]{1,0:T(8,128)}, u32[]{:S(2)}) copy-start(f32[256,128]{1,0:T(8,128)} %param.7) | copy-start | bytes 393220
  65.2 4.5 %copy-start.2 = (f32[256]{0:T(256)S(1)}, f32[256]{0:T(256)}, u32[]{:S(2)}) copy-start(f32[256]{0:T(256)} %param.8) | copy-start | bytes 3076
  69.8 86.0 %copy-start.1 = (f32[256,128]{1,0:T(8,128)}, f32[256,128]{1,0:T(8,128)S(1)}, u32[]{:S(2)}) copy-start(f32[256,128]{1,0:T(8,128)S(1)} %multiply_add_fusion) | copy-start | bytes 393220
Sparse Core Ops, SparseCore 0:
  10.2 44.0 all-gather.1
  71.0 83.2 all-reduce.1
where the time goes:
time: 164 us; the launch traced here: 163 us
  waiting for transfers between devices  123 us (75%)
  between operations  14.8 us (9%)
  local copies, waits for them, and re-layouts  12.5 us (8%)
  matrix products  11.9 us (7%)
    psum x1, waiting for transfers between devices, shards(): reduced = lax.psum(partial_term, 'row')  83.4 us
    all_gather x1, waiting for transfers between devices, shards(): gathered = lax.all_gather(own_blocks, 'row', axis=0, tiled=True)  39.2 us
    dot_general x1, matrix products, shards(): jnp.einsum('sij,sjk->sik', square_blocks, picked, precision=lax.Precision...  6.52 us
    reshape x1, local copies, waits for them, and re-layouts, shards(): square_blocks = tangent_blocks.reshape(CAP, B, B)  4.52 us
    gather x1, local copies, waits for them, and re-layouts, shards(): picked = gathered[owner_ids * BR_DEV + tile_offset]  4.35 us
    dot_general x1, matrix products, shards(): jnp.dot(row_select, products.reshape(CAP, B * MODES), precision=lax.Preci...  4.34 us
    unnamed x14, local copies, waits for them, and re-layouts  3.52 us
  transfers between devices with their start and end apart: 2, of which 2 were waited for; matrix products, arithmetic and copies ran while one was open for 4% of the time, Pallas kernels for 0%

commit v1 on v0

v1 whole, which is shorter than its diff:
```python
import functools

import jax
import jax.numpy as jnp
from jax import lax
from jax.experimental import pallas as pl
from jax.experimental.pallas import tpu as pltpu
from jax.sharding import PartitionSpec as P

B = 64
MODES = 128
BR_DEV = 4
CAP = 128
LINKS = 8
HALF = B // 2
ROWS = BR_DEV * B


def split(x):
    high = x.astype(jnp.bfloat16)
    return high, (x - high.astype(jnp.float32)).astype(jnp.bfloat16)


def dot3(a_high, a_low, b_high, b_low):
    dot = functools.partial(jnp.dot, preferred_element_type=jnp.float32)
    return dot(a_high, b_high) + (dot(a_low, b_high) + dot(a_high, b_low))


def assemble(place_ref, count_ref, blocks_ref, basis_ref, high_ref, low_ref, turned_high_ref, turned_low_ref, slots, dense):
    @pl.loop(0, CAP // 8)
    def _(group):
        eight = blocks_ref[pl.ds(pl.multiple_of(group * 8, 8), 8), :]
        for t in range(HALF):
            slots[pl.ds(group * (8 * HALF) + t, 8, stride=HALF), :] = eight[:, t * 128:(t + 1) * 128]

    dense[...] = jnp.zeros_like(dense)

    @pl.loop(0, count_ref[0])
    def _(s):
        target = pl.ds(pl.multiple_of(place_ref[s] * HALF, HALF), HALF)
        dense[target, :] += slots[pl.ds(pl.multiple_of(s * HALF, HALF), HALF), :]

    left = lax.broadcasted_iota(jnp.int32, (HALF, 128), 1) < B

    @pl.loop(0, LINKS)
    def _(link):
        for r in range(BR_DEV):
            for pair in range(BR_DEV // 2):
                start = ((link * BR_DEV + r) * BR_DEV + 2 * pair) * HALF
                first = dense[pl.ds(pl.multiple_of(start, HALF), HALF), :]
                second = dense[pl.ds(pl.multiple_of(start + HALF, HALF), HALF), :]
                even = jnp.where(left, first, pltpu.roll(second, B, 1))
                odd = jnp.where(left, pltpu.roll(first, B, 1), second)
                for h, part in enumerate((even, odd)):
                    high, low = split(part)
                    rows = slice(r * B + h * HALF, r * B + (h + 1) * HALF)
                    high_ref[link, rows, pair * 128:(pair + 1) * 128] = high
                    low_ref[link, rows, pair * 128:(pair + 1) * 128] = low

    high, low = split(basis_ref[...].T)
    turned_high_ref[...] = high
    turned_low_ref[...] = low


def project(scale, high_ref, low_ref, turned_high_ref, turned_low_ref, base_ref, *refs):
    basis_refs, (stiff_ref, partial_ref) = refs[:LINKS], refs[LINKS:]
    total = jnp.zeros((ROWS, MODES), jnp.float32)
    for link in range(LINKS):
        b_high, b_low = split(basis_refs[link][...])
        total += dot3(high_ref[link], low_ref[link], b_high, b_low)
    for r in range(BR_DEV):
        for h in range(2):
            rows = pl.ds(r * B + h, HALF, stride=2)
            start = r * B + h * HALF
            stiff_ref[rows, :] = base_ref[rows, :] + total[start:start + HALF, :]
    s_high, s_low = split(stiff_ref[...])
    partial_ref[...] = dot3(turned_high_ref[...], turned_low_ref[...], s_high, s_low) * scale


def shards(basis, springs, tangent_blocks, tile_rows, tile_owner, tile_offset, tile_count):
    n = lax.axis_size("row")
    me = lax.axis_index("row")
    steps = (0, 1, n - 1, 4, n - 4, 5, n - 5, n // 2)
    held = [basis]
    for step in steps[1:]:
        held.append(lax.ppermute(basis, "row", [((d + step) % n, d) for d in range(n)]))

    away = (tile_owner[:, 0] - me + n) % n
    link = jnp.zeros_like(away)
    for k, step in enumerate(steps):
        link = jnp.where(away == step, k, link)
    place = (link * BR_DEV + tile_rows) * BR_DEV + tile_offset

    smem = pl.BlockSpec(memory_space=pltpu.SMEM)
    vmem = pl.BlockSpec(memory_space=pltpu.VMEM)
    half = jnp.bfloat16
    high, low, turned_high, turned_low = pl.pallas_call(
        assemble,
        out_shape=(
            jax.ShapeDtypeStruct((LINKS, ROWS, ROWS), half),
            jax.ShapeDtypeStruct((LINKS, ROWS, ROWS), half),
            jax.ShapeDtypeStruct((MODES, ROWS), half),
            jax.ShapeDtypeStruct((MODES, ROWS), half),
        ),
        in_specs=[smem, smem, vmem, vmem],
        out_specs=(vmem,) * 4,
        scratch_shapes=[pltpu.VMEM((CAP * HALF, 128), jnp.float32), pltpu.VMEM((CAP * HALF, 128), jnp.float32)],
        compiler_params=pltpu.CompilerParams(vmem_limit_bytes=32 * 2**20),
        cost_estimate=pl.CostEstimate(flops=10_000_000, bytes_accessed=12_000_000, transcendentals=0),
        name="assemble",
    )(place, tile_count, tangent_blocks, basis)

    base = springs[:, None] * basis
    stiff_image, partial = pl.pallas_call(
        functools.partial(project, 1.0 / (basis.shape[0] * n)),
        out_shape=(
            jax.ShapeDtypeStruct((ROWS, MODES), jnp.float32),
            jax.ShapeDtypeStruct((MODES, MODES), jnp.float32),
        ),
        in_specs=[vmem] * (5 + LINKS),
        out_specs=(vmem,) * 2,
        compiler_params=pltpu.CompilerParams(vmem_limit_bytes=32 * 2**20),
        cost_estimate=pl.CostEstimate(flops=6 * 67_000_000, bytes_accessed=4_000_000, transcendentals=0),
        name="project",
    )(high, low, turned_high, turned_low, base, *held)

    pieces = partial.reshape(n, MODES // n, MODES)
    mine = lax.all_to_all(pieces, "row", 0, 0).sum(axis=0)
    whole = lax.all_to_all(jnp.broadcast_to(mine[None], pieces.shape), "row", 0, 0)
    return (stiff_image, whole.reshape(MODES, MODES))


def solution(mesh):
    in_specs = (
        P(("groups", "row"), None),
        P(("groups", "row")),
        P(("groups", "row"), None),
        P(("groups", "row")),
        P(("groups", "row"), None),
        P(("groups", "row")),
        P(("groups", "row")),
    )
    out_specs = (P(("groups", "row"), None), P("groups", None))
    return jax.shard_map(shards, mesh=mesh, in_specs=in_specs, out_specs=out_specs, check_vma=False)
```

time: 164 us -> 50.7 us (0.31)
  waiting for transfers between devices: 123 us -> 6.7 us
  blocking collectives: 0 us -> 19.8 us
  between operations: 14.8 us -> 1.36 us
  starting transfers between devices: 0.08 us -> 13.3 us
  matrix products: 11.9 us -> 0 us
  local copies, waits for them, and re-layouts: 12.5 us -> 3.14 us
  Pallas kernels: 0 us -> 5.13 us
    psum x1 -> x0, waiting for transfers between devices: 83.4 us -> none  [shards(): reduced = lax.psum(partial_term, 'row')]
    all_gather x1 -> x0, waiting for transfers between devices: 39.2 us -> none  [shards(): gathered = lax.all_gather(own_blocks, 'row', axis=0, tiled=True)]
    all_to_all x0 -> x2, blocking collectives: none -> 19.8 us  [the longest x1 10.4 us: shards(): mine = lax.all_to_all(pieces, 'row', 0, 0).sum(axis=0)]
    ppermute x0 -> x7, starting transfers between devices: none -> 13.3 us  [shards(): lax.ppermute(basis, 'row', [((d + step) % n, d) for d in range(n)])]
    dot_general x3 -> x0, matrix products: 11.9 us -> none  [the longest x1 6.52 us: shards(): jnp.einsum('sij,sjk->sik', square_blocks, picked, precision=lax.Precision...]
    ppermute x0 -> x7, waiting for transfers between devices: none -> 6.7 us  [shards(): lax.ppermute(basis, 'row', [((d + step) % n, d) for d in range(n)])]
    pallas_call x0 -> x2, Pallas kernels: none -> 5.13 us  [the longest x1 3.42 us: shards(): pl.pallas_call(assemble, out_shape=(jax.ShapeDtypeStruct((LINKS, ROWS, RO...]
    reshape x2 -> x0, local copies, waits for them, and re-layouts: 4.62 us -> none  [the longest x1 4.52 us: shards(): square_blocks = tangent_blocks.reshape(CAP, B, B)]
  transfers between devices with their start and end apart: 2 -> 7, of which waited for: 2 -> 2; matrix products, arithmetic and copies ran while one was open for 4% -> 2% of each run, Pallas kernels for 0% -> 7%
where the time goes in v1:
time: 50.7 us; the launch traced here: 50.3 us
  blocking collectives  19.8 us (39%)
  starting transfers between devices  13.3 us (26%)
  waiting for transfers between devices  6.7 us (13%)
  Pallas kernels  5.13 us (10%)
  local copies, waits for them, and re-layouts  3.14 us (6%)
  between operations  1.36 us (3%)
  other arithmetic  0.82 us (2%)
    ppermute x7, starting transfers between devices, shards(): lax.ppermute(basis, 'row', [((d + step) % n, d) for d in range(n)])  13.3 us
    all_to_all x1, blocking collectives, shards(): mine = lax.all_to_all(pieces, 'row', 0, 0).sum(axis=0)  10.4 us
    all_to_all x1, blocking collectives, shards(): lax.all_to_all(jnp.broadcast_to(mine[None], pieces.shape), 'row', 0, 0)  9.48 us
    ppermute x7, waiting for transfers between devices, shards(): lax.ppermute(basis, 'row', [((d + step) % n, d) for d in range(n)])  6.7 us
    pallas_call x1, Pallas kernels, shards(): pl.pallas_call(assemble, out_shape=(jax.ShapeDtypeStruct((LINKS, ROWS, RO...  3.42 us
    unnamed x9, local copies, waits for them, and re-layouts  3.13 us
    pallas_call x1, Pallas kernels, shards(): pl.pallas_call(functools.partial(project, 1.0 / (basis.shape[0] * n)), ou...  1.71 us
  transfers between devices with their start and end apart: 7, of which 2 were waited for; matrix products, arithmetic and copies ran while one was open for 2% of the time, Pallas kernels for 7%

profile of v1, /device:TPU:0, one launch (start us, length us, event | category | flops | bytes accessed | tf_op | source)
XLA Modules:
  0.0 50.3 jit_solution(16007238785651943048)
XLA Ops:
  0.6 0.0 copy-start.3
  0.6 2.5 %collective-permute-start.5 = (f32[256,128]{1,0:T(8,128)}, f32[256,128]{1,0:T(8,128)S(1)}, u32[]{:S(2)}, u32[]{:S(2)}) collective-permute-start(f32[256,128]{1,0:T(8,128)} %refs_0_.1), channel_id=1, source_target_pairs={{11,0},{12,1},{13,2},{14,3},{15,4},{0,5},{1,6},{2,7},{3,8},{4,9},{... | collective-permute-start | bytes 393224 | tf_op jit(solution)/shard_map/ppermute | solution.py:86
  3.2 2.0 %collective-permute-start.4 = (f32[256,128]{1,0:T(8,128)}, f32[256,128]{1,0:T(8,128)S(1)}, u32[]{:S(2)}, u32[]{:S(2)}) collective-permute-start(f32[256,128]{1,0:T(8,128)} %refs_0_.1), channel_id=1, source_target_pairs={{5,0},{6,1},{7,2},{8,3},{9,4},{10,5},{11,6},{12,7},{13,8},{14,9},{... | collective-permute-start | bytes 393224 | tf_op jit(solution)/shard_map/ppermute | solution.py:86
  5.2 2.1 %collective-permute-start.3 = (f32[256,128]{1,0:T(8,128)}, f32[256,128]{1,0:T(8,128)S(1)}, u32[]{:S(2)}, u32[]{:S(2)}) collective-permute-start(f32[256,128]{1,0:T(8,128)} %refs_0_.1), channel_id=1, source_target_pairs={{12,0},{13,1},{14,2},{15,3},{0,4},{1,5},{2,6},{3,7},{4,8},{5,9},{6... | collective-permute-start | bytes 393224 | tf_op jit(solution)/shard_map/ppermute | solution.py:86
  7.3 2.0 %collective-permute-start.2 = (f32[256,128]{1,0:T(8,128)}, f32[256,128]{1,0:T(8,128)S(1)}, u32[]{:S(2)}, u32[]{:S(2)}) collective-permute-start(f32[256,128]{1,0:T(8,128)} %refs_0_.1), channel_id=1, source_target_pairs={{4,0},{5,1},{6,2},{7,3},{8,4},{9,5},{10,6},{11,7},{12,8},{13,9},{1... | collective-permute-start | bytes 393224 | tf_op jit(solution)/shard_map/ppermute | solution.py:86
  9.3 0.0 collective-permute-start.1
  9.9 0.7 %multiply_add_fusion.place_ref = s32[128]{0:T(128)S(1)} fusion(s32[128]{0:T(128)} %param.12, s32[128]{0:T(128)} %param.10, s32[128,1]{0,1:T(1,128)} %param.11, s32[]{:T(128)S(6)} %axis_index.12), kind=kLoop, calls=%fused_computation.14 | loop fusion | flops 3968 | bytes 2052 | tf_op jit(solution)/shard_map/add | solution.py:92
  10.7 0.0 copy-start
  10.7 1.6 %copy-done = f32[128,4096]{1,0:T(8,128)S(1)} copy-done((f32[128,4096]{1,0:T(8,128)S(1)}, f32[128,4096]{1,0:T(8,128)}, u32[]{:S(2)}) %copy-start) | copy-done | bytes 2097176
  12.2 0.0 copy-start.1
  12.3 0.9 %copy-done.1 = f32[256,128]{1,0:T(8,128)S(1)} copy-done((f32[256,128]{1,0:T(8,128)S(1)}, f32[256,128]{1,0:T(8,128)}, u32[]{:S(2)}) %copy-start.1) | copy-done | bytes 131096
  13.2 0.0 copy-start.2
  13.2 3.4 %assemble.1 = (bf16[8,256,256]{2,1,0:T(8,128)(2,1)S(1)}, bf16[8,256,256]{2,1,0:T(8,128)(2,1)S(1)}, bf16[128,256]{1,0:T(8,128)(2,1)S(1)}, bf16[128,256]{1,0:T(8,128)(2,1)S(1)}) custom-call(s32[128]{0:T(128)S(1)} %multiply_add_fusion.place_ref, s32[1]{0:T(128)S(6)} %copy.10.count_ref, f32[128,4096]{1,0:T(8,128)S(1)} %copy-done, f32[256,128]{1,0:T(8,128)S(1)} %copy-done.1), custom_call_target="tpu_custom_call" | custom-call | flops 10000000 | bytes 12000000 | tf_op jit(solution)/shard_map/assemble/pallas_call | solution.py:97
  16.6 0.0 collective-permute-done.5.refs_6_
  16.6 4.7 %collective-permute-start = (f32[256,128]{1,0:T(8,128)S(1)}, f32[256,128]{1,0:T(8,128)S(1)}, u32[]{:S(2)}, u32[]{:S(2)}) collective-permute-start(f32[256,128]{1,0:T(8,128)S(1)} %copy-done.1), channel_id=1, source_target_pairs={{1,0},{2,1},{3,2},{4,3},{5,4},{6,5},{7,6},{8,7},{9,8},{10,9},{11,1... | collective-permute-start | bytes 393224 | tf_op jit(solution)/shard_map/ppermute | solution.py:86
  21.3 0.0 collective-permute-done.4.refs_5_
  21.3 0.0 collective-permute-start.6
  21.3 0.0 copy-done.3
  21.3 0.1 broadcast_multiply_fusion.base_ref
  21.4 0.0 collective-permute-done.3.refs_4_
  21.4 0.0 collective-permute-done.2.refs_3_
  21.4 0.0 collective-permute-done.1.refs_2_
  21.4 2.4 %collective-permute-done.refs_1_ = f32[256,128]{1,0:T(8,128)S(1)} collective-permute-done((f32[256,128]{1,0:T(8,128)S(1)}, f32[256,128]{1,0:T(8,128)S(1)}, u32[]{:S(2)}, u32[]{:S(2)}) %collective-permute-start) | collective-permute-done | bytes 131104 | tf_op jit(solution)/shard_map/ppermute | solution.py:86
  23.8 4.3 %collective-permute-done.6.refs_7_ = f32[256,128]{1,0:T(8,128)S(1)} collective-permute-done((f32[256,128]{1,0:T(8,128)S(1)}, f32[256,128]{1,0:T(8,128)S(1)}, u32[]{:S(2)}, u32[]{:S(2)}) %collective-permute-start.6) | collective-permute-done | bytes 131104 | tf_op jit(solution)/shard_map/ppermute | solution.py:86
  28.1 0.0 copy-done.2
  28.1 1.7 %project.1 = (f32[256,128]{1,0:T(8,128)}, f32[128,128]{1,0:T(8,128)S(1)}) custom-call(bf16[8,256,256]{2,1,0:T(8,128)(2,1)S(1)} %get-tuple-element.8.high_ref, bf16[8,256,256]{2,1,0:T(8,128)(2,1)S(1)} %get-tuple-element.9.low_ref, bf16[128,256]{1,0:T(8,128)(2,1)S(1)} %get-tuple-element.10.turned_high_ref, ...), custom_call_target="tpu_custom_call" | custom-call | flops 402000000 | bytes 4000000 | tf_op jit(solution)/shard_map/project/pallas_call | solution.py:114
  29.8 10.4 %all_to_all.10 = f32[16,8,128]{2,1,0:T(8,128)S(1)} all-to-all(f32[16,8,128]{2,1,0:T(8,128)S(1)} %bitcast.6), channel_id=1, replica_groups=mesh['groups'=2,'row'=16] {'row'}, dimensions={0} | all-to-all | bytes 131072 | tf_op jit(solution)/shard_map/all_to_all | solution.py:128
  40.2 9.5 %all_to_all.11 = f32[16,8,128]{2,1,0:T(8,128)S(1)} all-to-all(f32[16,8,128]{2,1,0:T(8,128)S(1)} %broadcast_in_dim.31), channel_id=1, replica_groups=mesh['groups'=2,'row'=16] {'row'}, dimensions={0} | all-to-all | bytes 131072 | tf_op jit(solution)/shard_map/all_to_all | solution.py:129
  49.7 0.6 %copy.11 = f32[128,128]{1,0:T(8,128)} copy(f32[128,128]{1,0:T(8,128)S(1)} %bitcast.7) | data formatting | bytes 131072
  (2 shorter events, 0.0 us)
Async XLA Ops:
  0.6 20.7 %copy-start.3 = (f32[256]{0:T(256)S(1)}, f32[256]{0:T(256)}, u32[]{:S(2)}) copy-start(f32[256]{0:T(256)} %param.8) | copy-start | bytes 3076
  0.6 15.9 %collective-permute-start.5 = (f32[256,128]{1,0:T(8,128)}, f32[256,128]{1,0:T(8,128)S(1)}, u32[]{:S(2)}, u32[]{:S(2)}) collective-permute-start(f32[256,128]{1,0:T(8,128)} %refs_0_.1), channel_id=1, source_target_pairs={{11,0},{12,1},{13,2},{14,3},{15,4},{0,5},{1,6},{2,7},{3,8},{4,9},{... | collective-permute-start | bytes 393224 | tf_op jit(solution)/shard_map/ppermute | solution.py:86
  3.2 18.1 %collective-permute-start.4 = (f32[256,128]{1,0:T(8,128)}, f32[256,128]{1,0:T(8,128)S(1)}, u32[]{:S(2)}, u32[]{:S(2)}) collective-permute-start(f32[256,128]{1,0:T(8,128)} %refs_0_.1), channel_id=1, source_target_pairs={{5,0},{6,1},{7,2},{8,3},{9,4},{10,5},{11,6},{12,7},{13,8},{14,9},{... | collective-permute-start | bytes 393224 | tf_op jit(solution)/shard_map/ppermute | solution.py:86
  5.2 16.2 %collective-permute-start.3 = (f32[256,128]{1,0:T(8,128)}, f32[256,128]{1,0:T(8,128)S(1)}, u32[]{:S(2)}, u32[]{:S(2)}) collective-permute-start(f32[256,128]{1,0:T(8,128)} %refs_0_.1), channel_id=1, source_target_pairs={{12,0},{13,1},{14,2},{15,3},{0,4},{1,5},{2,6},{3,7},{4,8},{5,9},{6... | collective-permute-start | bytes 393224 | tf_op jit(solution)/shard_map/ppermute | solution.py:86
  7.3 14.1 %collective-permute-start.2 = (f32[256,128]{1,0:T(8,128)}, f32[256,128]{1,0:T(8,128)S(1)}, u32[]{:S(2)}, u32[]{:S(2)}) collective-permute-start(f32[256,128]{1,0:T(8,128)} %refs_0_.1), channel_id=1, source_target_pairs={{4,0},{5,1},{6,2},{7,3},{8,4},{9,5},{10,6},{11,7},{12,8},{13,9},{1... | collective-permute-start | bytes 393224 | tf_op jit(solution)/shard_map/ppermute | solution.py:86
  9.3 12.1 %collective-permute-start.1 = (f32[256,128]{1,0:T(8,128)}, f32[256,128]{1,0:T(8,128)S(1)}, u32[]{:S(2)}, u32[]{:S(2)}) collective-permute-start(f32[256,128]{1,0:T(8,128)} %refs_0_.1), channel_id=1, source_target_pairs={{15,0},{0,1},{1,2},{2,3},{3,4},{4,5},{5,6},{6,7},{7,8},{8,9},{9,10... | collective-permute-start | bytes 393224 | tf_op jit(solution)/shard_map/ppermute | solution.py:86
  10.7 1.6 %copy-start = (f32[128,4096]{1,0:T(8,128)S(1)}, f32[128,4096]{1,0:T(8,128)}, u32[]{:S(2)}) copy-start(f32[128,4096]{1,0:T(8,128)} %blocks_ref.1) | copy-start | bytes 6291460
  12.2 0.9 %copy-start.1 = (f32[256,128]{1,0:T(8,128)S(1)}, f32[256,128]{1,0:T(8,128)}, u32[]{:S(2)}) copy-start(f32[256,128]{1,0:T(8,128)} %refs_0_.1) | copy-start | bytes 393220
  13.2 15.0 %copy-start.2 = (f32[256,128]{1,0:T(8,128)S(1)}, f32[256,128]{1,0:T(8,128)}, u32[]{:S(2)}) copy-start(f32[256,128]{1,0:T(8,128)} %refs_0_.1) | copy-start | bytes 393220
  16.6 7.2 %collective-permute-start = (f32[256,128]{1,0:T(8,128)S(1)}, f32[256,128]{1,0:T(8,128)S(1)}, u32[]{:S(2)}, u32[]{:S(2)}) collective-permute-start(f32[256,128]{1,0:T(8,128)S(1)} %copy-done.1), channel_id=1, source_target_pairs={{1,0},{2,1},{3,2},{4,3},{5,4},{6,5},{7,6},{8,7},{9,8},{10,9},{11,1... | collective-permute-start | bytes 393224 | tf_op jit(solution)/shard_map/ppermute | solution.py:86
  21.3 6.8 %collective-permute-start.6 = (f32[256,128]{1,0:T(8,128)S(1)}, f32[256,128]{1,0:T(8,128)S(1)}, u32[]{:S(2)}, u32[]{:S(2)}) collective-permute-start(f32[256,128]{1,0:T(8,128)S(1)} %copy-done.1), channel_id=1, source_target_pairs={{8,0},{9,1},{10,2},{11,3},{12,4},{13,5},{14,6},{15,7},{0,8},{1,9},... | collective-permute-start | bytes 393224 | tf_op jit(solution)/shard_map/ppermute | solution.py:86

commit v2 on v1

--- a/solution.py
+++ b/solution.py
@@ -124,10 +124,12 @@
         name="project",
     )(high, low, turned_high, turned_low, base, *held)
 
-    pieces = partial.reshape(n, MODES // n, MODES)
-    mine = lax.all_to_all(pieces, "row", 0, 0).sum(axis=0)
-    whole = lax.all_to_all(jnp.broadcast_to(mine[None], pieces.shape), "row", 0, 0)
-    return (stiff_image, whole.reshape(MODES, MODES))
+    reduced = partial
+    apart = 1
+    while apart < n:
+        reduced += lax.ppermute(reduced, "row", [(d, d ^ apart) for d in range(n)])
+        apart *= 2
+    return (stiff_image, reduced)
 
 
 def solution(mesh):

time: 50.7 us -> 45.9 us (0.905)
  blocking collectives: 19.8 us -> 0 us
  waiting for transfers between devices: 6.7 us -> 19.7 us
  starting transfers between devices: 13.3 us -> 15.3 us
  other arithmetic: 0.82 us -> 1.47 us
  local copies, waits for them, and re-layouts: 3.14 us -> 2.5 us
    all_to_all x2 -> x0, blocking collectives: 19.8 us -> none  [the longest x1 10.4 us: shards(): mine = lax.all_to_all(pieces, 'row', 0, 0).sum(axis=0)]
    ppermute x0 -> x4, waiting for transfers between devices: none -> 13.2 us  [shards(): reduced += lax.ppermute(reduced, 'row', [(d, d ^ apart) for d in range(n)])]
    ppermute x0 -> x4, starting transfers between devices: none -> 2.22 us  [shards(): reduced += lax.ppermute(reduced, 'row', [(d, d ^ apart) for d in range(n)])]
    add x0 -> x4, other arithmetic: none -> 0.67 us  [shards(): reduced += lax.ppermute(reduced, 'row', [(d, d ^ apart) for d in range(n)])]
    unnamed x9 -> x8, local copies, waits for them, and re-layouts: 3.13 us -> 2.5 us
  transfers between devices with their start and end apart: 7 -> 11, of which waited for: 2 -> 6; matrix products, arithmetic and copies ran while one was open for 2% -> 2% of each run, Pallas kernels for 7% -> 8%
where the time goes in v2:
time: 45.9 us; the launch traced here: 45.7 us
  waiting for transfers between devices  19.7 us (43%)
  starting transfers between devices  15.3 us (33%)
  Pallas kernels  5.33 us (12%)
  local copies, waits for them, and re-layouts  2.5 us (5%)
  other arithmetic  1.47 us (3%)
  between operations  1.38 us (3%)
    ppermute x4, waiting for transfers between devices, shards(): reduced += lax.ppermute(reduced, 'row', [(d, d ^ apart) for d in range(n)])  13.2 us
    ppermute x7, starting transfers between devices, shards(): lax.ppermute(basis, 'row', [((d + step) % n, d) for d in range(n)])  13.1 us
    ppermute x7, waiting for transfers between devices, shards(): lax.ppermute(basis, 'row', [((d + step) % n, d) for d in range(n)])  6.43 us
    pallas_call x1, Pallas kernels, shards(): pl.pallas_call(assemble, out_shape=(jax.ShapeDtypeStruct((LINKS, ROWS, RO...  3.62 us
    unnamed x8, local copies, waits for them, and re-layouts  2.5 us
    ppermute x4, starting transfers between devices, shards(): reduced += lax.ppermute(reduced, 'row', [(d, d ^ apart) for d in range(n)])  2.22 us
    pallas_call x1, Pallas kernels, shards(): pl.pallas_call(functools.partial(project, 1.0 / (basis.shape[0] * n)), ou...  1.71 us
  transfers between devices with their start and end apart: 11, of which 6 were waited for; matrix products, arithmetic and copies ran while one was open for 2% of the time, Pallas kernels for 8%

profile of v2, /device:TPU:0, one launch (start us, length us, event | category | flops | bytes accessed | tf_op | source)
XLA Modules:
  0.0 45.7 jit_solution(17559003549999286999)
XLA Ops:
  0.6 0.0 copy-start.3
  0.6 2.5 %collective-permute-start.5 = (f32[256,128]{1,0:T(8,128)}, f32[256,128]{1,0:T(8,128)S(1)}, u32[]{:S(2)}, u32[]{:S(2)}) collective-permute-start(f32[256,128]{1,0:T(8,128)} %refs_0_.1), channel_id=1, source_target_pairs={{11,0},{12,1},{13,2},{14,3},{15,4},{0,5},{1,6},{2,7},{3,8},{4,9},{... | collective-permute-start | bytes 393224 | tf_op jit(solution)/shard_map/ppermute | solution.py:86
  3.2 2.0 %collective-permute-start.4 = (f32[256,128]{1,0:T(8,128)}, f32[256,128]{1,0:T(8,128)S(1)}, u32[]{:S(2)}, u32[]{:S(2)}) collective-permute-start(f32[256,128]{1,0:T(8,128)} %refs_0_.1), channel_id=1, source_target_pairs={{5,0},{6,1},{7,2},{8,3},{9,4},{10,5},{11,6},{12,7},{13,8},{14,9},{... | collective-permute-start | bytes 393224 | tf_op jit(solution)/shard_map/ppermute | solution.py:86
  5.2 2.1 %collective-permute-start.3 = (f32[256,128]{1,0:T(8,128)}, f32[256,128]{1,0:T(8,128)S(1)}, u32[]{:S(2)}, u32[]{:S(2)}) collective-permute-start(f32[256,128]{1,0:T(8,128)} %refs_0_.1), channel_id=1, source_target_pairs={{12,0},{13,1},{14,2},{15,3},{0,4},{1,5},{2,6},{3,7},{4,8},{5,9},{6... | collective-permute-start | bytes 393224 | tf_op jit(solution)/shard_map/ppermute | solution.py:86
  7.3 2.0 %collective-permute-start.2 = (f32[256,128]{1,0:T(8,128)}, f32[256,128]{1,0:T(8,128)S(1)}, u32[]{:S(2)}, u32[]{:S(2)}) collective-permute-start(f32[256,128]{1,0:T(8,128)} %refs_0_.1), channel_id=1, source_target_pairs={{4,0},{5,1},{6,2},{7,3},{8,4},{9,5},{10,6},{11,7},{12,8},{13,9},{1... | collective-permute-start | bytes 393224 | tf_op jit(solution)/shard_map/ppermute | solution.py:86
  9.3 0.0 collective-permute-start.1
  9.9 0.7 %multiply_add_fusion.place_ref = s32[128]{0:T(128)S(1)} fusion(s32[128]{0:T(128)} %param.12, s32[128]{0:T(128)} %param.10, s32[128,1]{0,1:T(1,128)} %param.11, s32[]{:T(128)S(6)} %axis_index.12), kind=kLoop, calls=%fused_computation.14 | loop fusion | flops 3968 | bytes 2052 | tf_op jit(solution)/shard_map/add | solution.py:92
  10.7 0.0 copy-start
  10.7 1.6 %copy-done = f32[128,4096]{1,0:T(8,128)S(1)} copy-done((f32[128,4096]{1,0:T(8,128)S(1)}, f32[128,4096]{1,0:T(8,128)}, u32[]{:S(2)}) %copy-start) | copy-done | bytes 2097176
  12.3 0.9 %copy-done.1 = f32[256,128]{1,0:T(8,128)S(1)} copy-done((f32[256,128]{1,0:T(8,128)S(1)}, f32[256,128]{1,0:T(8,128)}, u32[]{:S(2)}) %copy-start.1) | copy-done | bytes 131096
  13.2 3.6 %assemble.1 = (bf16[8,256,256]{2,1,0:T(8,128)(2,1)S(1)}, bf16[8,256,256]{2,1,0:T(8,128)(2,1)S(1)}, bf16[128,256]{1,0:T(8,128)(2,1)S(1)}, bf16[128,256]{1,0:T(8,128)(2,1)S(1)}) custom-call(s32[128]{0:T(128)S(1)} %multiply_add_fusion.place_ref, s32[1]{0:T(128)S(6)} %copy.9.count_ref, f32[128,4096]{1,0:T(8,128)S(1)} %copy-done, f32[256,128]{1,0:T(8,128)S(1)} %copy-done.1), custom_call_target="tpu_custom_call" | custom-call | flops 10000000 | bytes 12000000 | tf_op jit(solution)/shard_map/assemble/pallas_call | solution.py:97
  16.8 0.0 collective-permute-done.5.refs_6_
  16.8 4.5 %collective-permute-start = (f32[256,128]{1,0:T(8,128)S(1)}, f32[256,128]{1,0:T(8,128)S(1)}, u32[]{:S(2)}, u32[]{:S(2)}) collective-permute-start(f32[256,128]{1,0:T(8,128)S(1)} %copy-done.1), channel_id=1, source_target_pairs={{1,0},{2,1},{3,2},{4,3},{5,4},{6,5},{7,6},{8,7},{9,8},{10,9},{11,1... | collective-permute-start | bytes 393224 | tf_op jit(solution)/shard_map/ppermute | solution.py:86
  21.3 0.0 collective-permute-done.4.refs_5_
  21.3 0.0 collective-permute-start.6
  21.3 0.0 copy-done.3
  21.3 0.1 broadcast_multiply_fusion.base_ref
  21.4 0.0 collective-permute-done.3.refs_4_
  21.4 0.0 collective-permute-done.2.refs_3_
  21.4 0.0 collective-permute-done.1.refs_2_
  21.4 2.4 %collective-permute-done.refs_1_ = f32[256,128]{1,0:T(8,128)S(1)} collective-permute-done((f32[256,128]{1,0:T(8,128)S(1)}, f32[256,128]{1,0:T(8,128)S(1)}, u32[]{:S(2)}, u32[]{:S(2)}) %collective-permute-start) | collective-permute-done | bytes 131104 | tf_op jit(solution)/shard_map/ppermute | solution.py:86
  23.8 4.0 %collective-permute-done.6.refs_7_ = f32[256,128]{1,0:T(8,128)S(1)} collective-permute-done((f32[256,128]{1,0:T(8,128)S(1)}, f32[256,128]{1,0:T(8,128)S(1)}, u32[]{:S(2)}, u32[]{:S(2)}) %collective-permute-start.6) | collective-permute-done | bytes 131104 | tf_op jit(solution)/shard_map/ppermute | solution.py:86
  27.8 1.7 %project.1 = (f32[256,128]{1,0:T(8,128)}, f32[128,128]{1,0:T(8,128)S(1)}) custom-call(bf16[8,256,256]{2,1,0:T(8,128)(2,1)S(1)} %get-tuple-element.8.high_ref, bf16[8,256,256]{2,1,0:T(8,128)(2,1)S(1)} %get-tuple-element.9.low_ref, bf16[128,256]{1,0:T(8,128)(2,1)S(1)} %get-tuple-element.10.turned_high_ref, ...), custom_call_target="tpu_custom_call" | custom-call | flops 402000000 | bytes 4000000 | tf_op jit(solution)/shard_map/project/pallas_call | solution.py:114
  29.5 0.0 collective-permute-start.7
  29.6 1.3 %collective-permute-done.7 = f32[128,128]{1,0:T(8,128)S(1)} collective-permute-done((f32[128,128]{1,0:T(8,128)S(1)}, f32[128,128]{1,0:T(8,128)S(1)}, u32[]{:S(2)}, u32[]{:S(2)}) %collective-permute-start.7) | collective-permute-done | bytes 65568 | tf_op jit(solution)/shard_map/ppermute | solution.py:130
  30.8 1.0 %collective-permute-start.8 = (f32[128,128]{1,0:T(8,128)S(1)}, f32[128,128]{1,0:T(8,128)S(1)}, u32[]{:S(2)}, u32[]{:S(2)}) collective-permute-start(f32[128,128]{1,0:T(8,128)S(1)} %add.42), channel_id=1, source_target_pairs={{0,2},{1,3},{2,0},{3,1},{4,6},{5,7},{6,4},{7,5},{8,10},{9,11},{10,... | collective-permute-start | bytes 196616 | tf_op jit(solution)/shard_map/ppermute | solution.py:130
  31.8 3.3 %collective-permute-done.8 = f32[128,128]{1,0:T(8,128)S(1)} collective-permute-done((f32[128,128]{1,0:T(8,128)S(1)}, f32[128,128]{1,0:T(8,128)S(1)}, u32[]{:S(2)}, u32[]{:S(2)}) %collective-permute-start.8) | collective-permute-done | bytes 65568 | tf_op jit(solution)/shard_map/ppermute | solution.py:130
  35.2 0.1 collective-permute-start.9
  35.2 4.3 %collective-permute-done.9 = f32[128,128]{1,0:T(8,128)S(1)} collective-permute-done((f32[128,128]{1,0:T(8,128)S(1)}, f32[128,128]{1,0:T(8,128)S(1)}, u32[]{:S(2)}, u32[]{:S(2)}) %collective-permute-start.9) | collective-permute-done | bytes 65568 | tf_op jit(solution)/shard_map/ppermute | solution.py:130
  39.5 1.1 %collective-permute-start.10 = (f32[128,128]{1,0:T(8,128)S(1)}, f32[128,128]{1,0:T(8,128)S(1)}, u32[]{:S(2)}, u32[]{:S(2)}) collective-permute-start(f32[128,128]{1,0:T(8,128)S(1)} %add.44), channel_id=1, source_target_pairs={{0,8},{1,9},{2,10},{3,11},{4,12},{5,13},{6,14},{7,15},{8,0},{9,1},... | collective-permute-start | bytes 196616 | tf_op jit(solution)/shard_map/ppermute | solution.py:130
  40.6 4.4 %collective-permute-done.10 = f32[128,128]{1,0:T(8,128)S(1)} collective-permute-done((f32[128,128]{1,0:T(8,128)S(1)}, f32[128,128]{1,0:T(8,128)S(1)}, u32[]{:S(2)}, u32[]{:S(2)}) %collective-permute-start.10) | collective-permute-done | bytes 65568 | tf_op jit(solution)/shard_map/ppermute | solution.py:130
  45.0 0.6 %add.45 = f32[128,128]{1,0:T(8,128)} add(f32[128,128]{1,0:T(8,128)S(1)} %add.44, f32[128,128]{1,0:T(8,128)S(1)} %collective-permute-done.10) | non-fusion elementwise | flops 16384 | bytes 196608 | tf_op jit(solution)/shard_map/add | solution.py:130
  (6 shorter events, 0.0 us)
Async XLA Ops:
  0.6 20.6 %copy-start.3 = (f32[256]{0:T(256)S(1)}, f32[256]{0:T(256)}, u32[]{:S(2)}) copy-start(f32[256]{0:T(256)} %param.8) | copy-start | bytes 3076
  0.6 16.1 %collective-permute-start.5 = (f32[256,128]{1,0:T(8,128)}, f32[256,128]{1,0:T(8,128)S(1)}, u32[]{:S(2)}, u32[]{:S(2)}) collective-permute-start(f32[256,128]{1,0:T(8,128)} %refs_0_.1), channel_id=1, source_target_pairs={{11,0},{12,1},{13,2},{14,3},{15,4},{0,5},{1,6},{2,7},{3,8},{4,9},{... | collective-permute-start | bytes 393224 | tf_op jit(solution)/shard_map/ppermute | solution.py:86
  3.2 18.1 %collective-permute-start.4 = (f32[256,128]{1,0:T(8,128)}, f32[256,128]{1,0:T(8,128)S(1)}, u32[]{:S(2)}, u32[]{:S(2)}) collective-permute-start(f32[256,128]{1,0:T(8,128)} %refs_0_.1), channel_id=1, source_target_pairs={{5,0},{6,1},{7,2},{8,3},{9,4},{10,5},{11,6},{12,7},{13,8},{14,9},{... | collective-permute-start | bytes 393224 | tf_op jit(solution)/shard_map/ppermute | solution.py:86
  5.2 16.2 %collective-permute-start.3 = (f32[256,128]{1,0:T(8,128)}, f32[256,128]{1,0:T(8,128)S(1)}, u32[]{:S(2)}, u32[]{:S(2)}) collective-permute-start(f32[256,128]{1,0:T(8,128)} %refs_0_.1), channel_id=1, source_target_pairs={{12,0},{13,1},{14,2},{15,3},{0,4},{1,5},{2,6},{3,7},{4,8},{5,9},{6... | collective-permute-start | bytes 393224 | tf_op jit(solution)/shard_map/ppermute | solution.py:86
  7.3 14.1 %collective-permute-start.2 = (f32[256,128]{1,0:T(8,128)}, f32[256,128]{1,0:T(8,128)S(1)}, u32[]{:S(2)}, u32[]{:S(2)}) collective-permute-start(f32[256,128]{1,0:T(8,128)} %refs_0_.1), channel_id=1, source_target_pairs={{4,0},{5,1},{6,2},{7,3},{8,4},{9,5},{10,6},{11,7},{12,8},{13,9},{1... | collective-permute-start | bytes 393224 | tf_op jit(solution)/shard_map/ppermute | solution.py:86
  9.3 12.1 %collective-permute-start.1 = (f32[256,128]{1,0:T(8,128)}, f32[256,128]{1,0:T(8,128)S(1)}, u32[]{:S(2)}, u32[]{:S(2)}) collective-permute-start(f32[256,128]{1,0:T(8,128)} %refs_0_.1), channel_id=1, source_target_pairs={{15,0},{0,1},{1,2},{2,3},{3,4},{4,5},{5,6},{6,7},{7,8},{8,9},{9,10... | collective-permute-start | bytes 393224 | tf_op jit(solution)/shard_map/ppermute | solution.py:86
  10.7 1.6 %copy-start = (f32[128,4096]{1,0:T(8,128)S(1)}, f32[128,4096]{1,0:T(8,128)}, u32[]{:S(2)}) copy-start(f32[128,4096]{1,0:T(8,128)} %blocks_ref.1) | copy-start | bytes 6291460
  12.2 0.9 %copy-start.1 = (f32[256,128]{1,0:T(8,128)S(1)}, f32[256,128]{1,0:T(8,128)}, u32[]{:S(2)}) copy-start(f32[256,128]{1,0:T(8,128)} %refs_0_.1) | copy-start | bytes 393220
  13.2 14.7 %copy-start.2 = (f32[256,128]{1,0:T(8,128)S(1)}, f32[256,128]{1,0:T(8,128)}, u32[]{:S(2)}) copy-start(f32[256,128]{1,0:T(8,128)} %refs_0_.1) | copy-start | bytes 393220
  16.8 7.0 %collective-permute-start = (f32[256,128]{1,0:T(8,128)S(1)}, f32[256,128]{1,0:T(8,128)S(1)}, u32[]{:S(2)}, u32[]{:S(2)}) collective-permute-start(f32[256,128]{1,0:T(8,128)S(1)} %copy-done.1), channel_id=1, source_target_pairs={{1,0},{2,1},{3,2},{4,3},{5,4},{6,5},{7,6},{8,7},{9,8},{10,9},{11,1... | collective-permute-start | bytes 393224 | tf_op jit(solution)/shard_map/ppermute | solution.py:86
  21.3 6.6 %collective-permute-start.6 = (f32[256,128]{1,0:T(8,128)S(1)}, f32[256,128]{1,0:T(8,128)S(1)}, u32[]{:S(2)}, u32[]{:S(2)}) collective-permute-start(f32[256,128]{1,0:T(8,128)S(1)} %copy-done.1), channel_id=1, source_target_pairs={{8,0},{9,1},{10,2},{11,3},{12,4},{13,5},{14,6},{15,7},{0,8},{1,9},... | collective-permute-start | bytes 393224 | tf_op jit(solution)/shard_map/ppermute | solution.py:86
  29.5 1.3 %collective-permute-start.7 = (f32[128,128]{1,0:T(8,128)S(1)}, f32[128,128]{1,0:T(8,128)S(1)}, u32[]{:S(2)}, u32[]{:S(2)}) collective-permute-start(f32[128,128]{1,0:T(8,128)S(1)} %get-tuple-element.13), channel_id=1, source_target_pairs={{0,1},{1,0},{2,3},{3,2},{4,5},{5,4},{6,7},{7,6},{8,9},{9,8},{10,11... | collective-permute-start | bytes 196616 | tf_op jit(solution)/shard_map/ppermute | solution.py:130
  30.8 4.3 %collective-permute-start.8 = (f32[128,128]{1,0:T(8,128)S(1)}, f32[128,128]{1,0:T(8,128)S(1)}, u32[]{:S(2)}, u32[]{:S(2)}) collective-permute-start(f32[128,128]{1,0:T(8,128)S(1)} %add.42), channel_id=1, source_target_pairs={{0,2},{1,3},{2,0},{3,1},{4,6},{5,7},{6,4},{7,5},{8,10},{9,11},{10,... | collective-permute-start | bytes 196616 | tf_op jit(solution)/shard_map/ppermute | solution.py:130
  35.2 4.3 %collective-permute-start.9 = (f32[128,128]{1,0:T(8,128)S(1)}, f32[128,128]{1,0:T(8,128)S(1)}, u32[]{:S(2)}, u32[]{:S(2)}) collective-permute-start(f32[128,128]{1,0:T(8,128)S(1)} %add.43), channel_id=1, source_target_pairs={{0,4},{1,5},{2,6},{3,7},{4,0},{5,1},{6,2},{7,3},{8,12},{9,13},{10,... | collective-permute-start | bytes 196616 | tf_op jit(solution)/shard_map/ppermute | solution.py:130
  39.5 5.5 %collective-permute-start.10 = (f32[128,128]{1,0:T(8,128)S(1)}, f32[128,128]{1,0:T(8,128)S(1)}, u32[]{:S(2)}, u32[]{:S(2)}) collective-permute-start(f32[128,128]{1,0:T(8,128)S(1)} %add.44), channel_id=1, source_target_pairs={{0,8},{1,9},{2,10},{3,11},{4,12},{5,13},{6,14},{7,15},{8,0},{9,1},... | collective-permute-start | bytes 196616 | tf_op jit(solution)/shard_map/ppermute | solution.py:130

commit v3 on v2

--- a/solution.py
+++ b/solution.py
@@ -12,6 +12,7 @@
 BR_DEV = 4
 CAP = 128
 LINKS = 8
+LATE = 3
 HALF = B // 2
 ROWS = BR_DEV * B
 
@@ -62,17 +63,30 @@
     turned_low_ref[...] = low
 
 
-def project(scale, high_ref, low_ref, turned_high_ref, turned_low_ref, base_ref, *refs):
-    basis_refs, (stiff_ref, partial_ref) = refs[:LINKS], refs[LINKS:]
+def project_early(high_ref, low_ref, springs_ref, own_ref, *refs):
+    basis_refs, total_ref = refs[:-1], refs[-1]
     total = jnp.zeros((ROWS, MODES), jnp.float32)
-    for link in range(LINKS):
-        b_high, b_low = split(basis_refs[link][...])
+    for link, ref in enumerate((own_ref,) + basis_refs):
+        b_high, b_low = split(ref[...])
         total += dot3(high_ref[link], low_ref[link], b_high, b_low)
     for r in range(BR_DEV):
         for h in range(2):
             rows = pl.ds(r * B + h, HALF, stride=2)
             start = r * B + h * HALF
-            stiff_ref[rows, :] = base_ref[rows, :] + total[start:start + HALF, :]
+            total_ref[rows, :] = springs_ref[rows, :] * own_ref[rows, :] + total[start:start + HALF, :]
+
+
+def project_late(scale, high_ref, low_ref, turned_high_ref, turned_low_ref, total_ref, *refs):
+    basis_refs, (stiff_ref, partial_ref) = refs[:LATE], refs[LATE:]
+    total = jnp.zeros((ROWS, MODES), jnp.float32)
+    for k, ref in enumerate(basis_refs):
+        b_high, b_low = split(ref[...])
+        total += dot3(high_ref[LINKS - LATE + k], low_ref[LINKS - LATE + k], b_high, b_low)
+    for r in range(BR_DEV):
+        for h in range(2):
+            rows = pl.ds(r * B + h, HALF, stride=2)
+            start = r * B + h * HALF
+            stiff_ref[rows, :] = total_ref[rows, :] + total[start:start + HALF, :]
     s_high, s_low = split(stiff_ref[...])
     partial_ref[...] = dot3(turned_high_ref[...], turned_low_ref[...], s_high, s_low) * scale
 
@@ -80,10 +94,15 @@
 def shards(basis, springs, tangent_blocks, tile_rows, tile_owner, tile_offset, tile_count):
     n = lax.axis_size("row")
     me = lax.axis_index("row")
-    steps = (0, 1, n - 1, 4, n - 4, 5, n - 5, n // 2)
-    held = [basis]
-    for step in steps[1:]:
-        held.append(lax.ppermute(basis, "row", [((d + step) % n, d) for d in range(n)]))
+    steps = (0, 1, n - 1, 4, n - 4, n // 2, 5, n - 5)
+
+    def fetch(block, step):
+        return lax.ppermute(block, "row", [((d + step) % n, d) for d in range(n)])
+
+    above, below = fetch(basis, 4), fetch(basis, n - 4)
+    across = fetch(basis, n // 2)
+    after, before = fetch(basis, 1), fetch(basis, n - 1)
+    far_above, far_below = fetch(above, 1), fetch(below, n - 1)
 
     away = (tile_owner[:, 0] - me + n) % n
     link = jnp.zeros_like(away)
@@ -110,19 +129,27 @@
         name="assemble",
     )(place, tile_count, tangent_blocks, basis)
 
-    base = springs[:, None] * basis
+    total = pl.pallas_call(
+        project_early,
+        out_shape=jax.ShapeDtypeStruct((ROWS, MODES), jnp.float32),
+        in_specs=[vmem] * (3 + LINKS - LATE),
+        out_specs=vmem,
+        compiler_params=pltpu.CompilerParams(vmem_limit_bytes=32 * 2**20),
+        cost_estimate=pl.CostEstimate(flops=4 * 67_000_000, bytes_accessed=2_500_000, transcendentals=0),
+        name="project_early",
+    )(high, low, springs[:, None], basis, after, before, above, below)
     stiff_image, partial = pl.pallas_call(
-        functools.partial(project, 1.0 / (basis.shape[0] * n)),
+        functools.partial(project_late, 1.0 / (basis.shape[0] * n)),
         out_shape=(
             jax.ShapeDtypeStruct((ROWS, MODES), jnp.float32),
             jax.ShapeDtypeStruct((MODES, MODES), jnp.float32),
         ),
-        in_specs=[vmem] * (5 + LINKS),
+        in_specs=[vmem] * (5 + LATE),
         out_specs=(vmem,) * 2,
         compiler_params=pltpu.CompilerParams(vmem_limit_bytes=32 * 2**20),
-        cost_estimate=pl.CostEstimate(flops=6 * 67_000_000, bytes_accessed=4_000_000, transcendentals=0),
-        name="project",
-    )(high, low, turned_high, turned_low, base, *held)
+        cost_estimate=pl.CostEstimate(flops=2 * 67_000_000, bytes_accessed=1_500_000, transcendentals=0),
+        name="project_late",
+    )(high, low, turned_high, turned_low, total, across, far_above, far_below)
 
     reduced = partial
     apart = 1

time: 45.9 us -> 41 us (0.89)
  waiting for transfers between devices: 19.7 us -> 11.7 us
  starting transfers between devices: 15.3 us -> 17.6 us
  local copies, waits for them, and re-layouts: 2.5 us -> 3.3 us
    ppermute x7, waiting for transfers between devices: 6.43 us -> 0.57 us  [fetch(): return lax.ppermute(block, 'row', [((d + step) % n, d) for d in range(n)])]
    ppermute x4, starting transfers between devices: 2.22 us -> 4.95 us  [shards(): reduced += lax.ppermute(reduced, 'row', [(d, d ^ apart) for d in range(n)])]
    ppermute x4, waiting for transfers between devices: 13.2 us -> 11.2 us  [shards(): reduced += lax.ppermute(reduced, 'row', [(d, d ^ apart) for d in range(n)])]
    broadcast_in_dim x0 -> x1, local copies, waits for them, and re-layouts: none -> 0.81 us  [shards(): springs[:, None]]
    ppermute x7, starting transfers between devices: 13.1 us -> 12.7 us  [fetch(): return lax.ppermute(block, 'row', [((d + step) % n, d) for d in range(n)])]
    pallas_call x1 -> x2, Pallas kernels: 1.71 us -> 1.87 us  [the longest x1 1.19 us: shards(): pl.pallas_call(functools.partial(project_late, 1.0 / (basis.shape[0] * n)...]
    unnamed x8 -> x4, local copies, waits for them, and re-layouts: 2.5 us -> 2.49 us
  transfers between devices with their start and end apart: 11 -> 11, of which waited for: 6 -> 5; matrix products, arithmetic and copies ran while one was open for 2% -> 4% of each run, Pallas kernels for 8% -> 11%
where the time goes in v3:
time: 41 us; the launch traced here: 41.1 us
  starting transfers between devices  17.6 us (43%)
  waiting for transfers between devices  11.7 us (29%)
  Pallas kernels  5.76 us (14%)
  local copies, waits for them, and re-layouts  3.3 us (8%)
  other arithmetic  1.37 us (3%)
  between operations  1.37 us (3%)
    ppermute x7, starting transfers between devices, fetch(): return lax.ppermute(block, 'row', [((d + step) % n, d) for d in range(n)])  12.7 us
    ppermute x4, waiting for transfers between devices, shards(): reduced += lax.ppermute(reduced, 'row', [(d, d ^ apart) for d in range(n)])  11.2 us
    ppermute x4, starting transfers between devices, shards(): reduced += lax.ppermute(reduced, 'row', [(d, d ^ apart) for d in range(n)])  4.95 us
    pallas_call x1, Pallas kernels, shards(): pl.pallas_call(assemble, out_shape=(jax.ShapeDtypeStruct((LINKS, ROWS, RO...  3.89 us
    unnamed x4, local copies, waits for them, and re-layouts  2.49 us
    pallas_call x1, Pallas kernels, shards(): pl.pallas_call(functools.partial(project_late, 1.0 / (basis.shape[0] * n)...  1.19 us
  transfers between devices with their start and end apart: 11, of which 5 were waited for; matrix products, arithmetic and copies ran while one was open for 4% of the time, Pallas kernels for 11%

profile of v3, /device:TPU:0, one launch (start us, length us, event | category | flops | bytes accessed | tf_op | source)
XLA Modules:
  0.0 41.1 jit_solution(14020769559233011743)
XLA Ops:
  0.6 5.1 %collective-permute-start.2 = (f32[256,128]{1,0:T(8,128)}, f32[256,128]{1,0:T(8,128)S(1)}, u32[]{:S(2)}, u32[]{:S(2)}) collective-permute-start(f32[256,128]{1,0:T(8,128)} %own_ref.1), channel_id=1, source_target_pairs={{4,0},{5,1},{6,2},{7,3},{8,4},{9,5},{10,6},{11,7},{12,8},{13,9},{1... | collective-permute-start | bytes 393224 | tf_op jit(solution)/shard_map/ppermute | solution.py:100
  5.7 0.0 collective-permute-start.3
  5.7 3.7 %collective-permute-start = (f32[256,128]{1,0:T(8,128)}, f32[256,128]{1,0:T(8,128)S(1)}, u32[]{:S(2)}, u32[]{:S(2)}) collective-permute-start(f32[256,128]{1,0:T(8,128)} %own_ref.1), channel_id=1, source_target_pairs={{1,0},{2,1},{3,2},{4,3},{5,4},{6,5},{7,6},{8,7},{9,8},{10,9},{11,1... | collective-permute-start | bytes 393224 | tf_op jit(solution)/shard_map/ppermute | solution.py:100
  9.4 0.0 collective-permute-start.1
  9.4 0.0 collective-permute-start.4
  9.4 0.6 %collective-permute-done.2.refs_2_ = f32[256,128]{1,0:T(8,128)S(1)} collective-permute-done((f32[256,128]{1,0:T(8,128)}, f32[256,128]{1,0:T(8,128)S(1)}, u32[]{:S(2)}, u32[]{:S(2)}) %collective-permute-start.2) | collective-permute-done | bytes 131104 | tf_op jit(solution)/shard_map/ppermute | solution.py:100
  10.0 3.9 %collective-permute-start.5 = (f32[256,128]{1,0:T(8,128)S(1)}, f32[256,128]{1,0:T(8,128)S(1)}, u32[]{:S(2)}, u32[]{:S(2)}) collective-permute-start(f32[256,128]{1,0:T(8,128)S(1)} %collective-permute-done.2.refs_2_), channel_id=1, source_target_pairs={{1,0},{2,1},{3,2},{4,3},{5,4},{6,5},{7,6},{8,7},{9,8},{10,9},{11,1... | collective-permute-start | bytes 393224 | tf_op jit(solution)/shard_map/ppermute | solution.py:100
  13.8 0.0 collective-permute-done.3.refs_3_
  13.8 0.0 collective-permute-start.6
  13.8 0.7 %multiply_add_fusion.place_ref = s32[128]{0:T(128)S(1)} fusion(s32[128]{0:T(128)} %param.12, s32[128]{0:T(128)} %param.10, s32[128,1]{0,1:T(1,128)} %param.11, s32[]{:T(128)S(6)} %axis_index.12), kind=kLoop, calls=%fused_computation.13 | loop fusion | flops 3968 | bytes 2052 | tf_op jit(solution)/shard_map/add | solution.py:111
  15.2 0.8 %copy.9.springs_ref = f32[256,1]{1,0:T(8,128)S(1)} copy(f32[256,1]{0,1:T(1,128)} %bitcast.5) | data formatting | bytes 2048 | tf_op jit(solution)/shard_map/broadcast_in_dim | solution.py:140
  16.0 0.0 copy-start
  16.0 1.6 %copy-done = f32[128,4096]{1,0:T(8,128)S(1)} copy-done((f32[128,4096]{1,0:T(8,128)S(1)}, f32[128,4096]{1,0:T(8,128)}, u32[]{:S(2)}) %copy-start) | copy-done | bytes 2097176
  17.6 0.0 copy-start.1
  17.6 0.9 %copy-done.1 = f32[256,128]{1,0:T(8,128)S(1)} copy-done((f32[256,128]{1,0:T(8,128)S(1)}, f32[256,128]{1,0:T(8,128)}, u32[]{:S(2)}) %copy-start.1) | copy-done | bytes 131096
  18.5 3.9 %assemble.1 = (bf16[8,256,256]{2,1,0:T(8,128)(2,1)S(1)}, bf16[8,256,256]{2,1,0:T(8,128)(2,1)S(1)}, bf16[128,256]{1,0:T(8,128)(2,1)S(1)}, bf16[128,256]{1,0:T(8,128)(2,1)S(1)}) custom-call(s32[128]{0:T(128)S(1)} %multiply_add_fusion.place_ref, s32[1]{0:T(128)S(6)} %copy.10.count_ref, f32[128,4096]{1,0:T(8,128)S(1)} %copy-done, f32[256,128]{1,0:T(8,128)S(1)} %copy-done.1), custom_call_target="tpu_custom_call" | custom-call | flops 10000000 | bytes 12000000 | tf_op jit(solution)/shard_map/assemble/pallas_call | solution.py:116
  22.4 0.0 collective-permute-done.refs_0_
  22.4 0.0 collective-permute-done.1.refs_1_
  22.4 0.7 %project_early.1.total_ref = f32[256,128]{1,0:T(8,128)S(1)} custom-call(bf16[8,256,256]{2,1,0:T(8,128)(2,1)S(1)} %get-tuple-element.8.high_ref, bf16[8,256,256]{2,1,0:T(8,128)(2,1)S(1)} %get-tuple-element.9.low_ref, f32[256,1]{1,0:T(8,128)S(1)} %copy.9.springs_ref, f32[256,128]{1,0:T(8,128)S(1)} %copy-done.1, f32[256,128]{1,0:T(8,128)S(1)} %collective-permute-done.refs_0_, ...), custom_call_target="tpu_custom_call" | custom-call | flops 268000000 | bytes 2500000 | tf_op jit(solution)/shard_map/project_early/pallas_call | solution.py:132
  23.1 0.0 collective-permute-done.4.refs_0_
  23.1 0.0 collective-permute-done.5.refs_1_
  23.1 0.0 collective-permute-done.6.refs_2_
  23.2 1.2 %project_late.1 = (f32[256,128]{1,0:T(8,128)}, f32[128,128]{1,0:T(8,128)S(1)}) custom-call(bf16[8,256,256]{2,1,0:T(8,128)(2,1)S(1)} %get-tuple-element.8.high_ref, bf16[8,256,256]{2,1,0:T(8,128)(2,1)S(1)} %get-tuple-element.9.low_ref, bf16[128,256]{1,0:T(8,128)(2,1)S(1)} %get-tuple-element.10.turned_high_ref, ...), custom_call_target="tpu_custom_call" | custom-call | flops 134000000 | bytes 1500000 | tf_op jit(solution)/shard_map/project_late/pallas_call | solution.py:141
  24.3 0.1 collective-permute-start.7
  24.4 1.2 %collective-permute-done.7 = f32[128,128]{1,0:T(8,128)S(1)} collective-permute-done((f32[128,128]{1,0:T(8,128)S(1)}, f32[128,128]{1,0:T(8,128)S(1)}, u32[]{:S(2)}, u32[]{:S(2)}) %collective-permute-start.7) | collective-permute-done | bytes 65568 | tf_op jit(solution)/shard_map/ppermute | solution.py:157
  25.6 2.7 %collective-permute-start.8 = (f32[128,128]{1,0:T(8,128)S(1)}, f32[128,128]{1,0:T(8,128)S(1)}, u32[]{:S(2)}, u32[]{:S(2)}) collective-permute-start(f32[128,128]{1,0:T(8,128)S(1)} %add.42), channel_id=1, source_target_pairs={{0,2},{1,3},{2,0},{3,1},{4,6},{5,7},{6,4},{7,5},{8,10},{9,11},{10,... | collective-permute-start | bytes 196616 | tf_op jit(solution)/shard_map/ppermute | solution.py:157
  28.3 2.6 %collective-permute-done.8 = f32[128,128]{1,0:T(8,128)S(1)} collective-permute-done((f32[128,128]{1,0:T(8,128)S(1)}, f32[128,128]{1,0:T(8,128)S(1)}, u32[]{:S(2)}, u32[]{:S(2)}) %collective-permute-start.8) | collective-permute-done | bytes 65568 | tf_op jit(solution)/shard_map/ppermute | solution.py:157
  30.9 1.3 %collective-permute-start.9 = (f32[128,128]{1,0:T(8,128)S(1)}, f32[128,128]{1,0:T(8,128)S(1)}, u32[]{:S(2)}, u32[]{:S(2)}) collective-permute-start(f32[128,128]{1,0:T(8,128)S(1)} %add.43), channel_id=1, source_target_pairs={{0,4},{1,5},{2,6},{3,7},{4,0},{5,1},{6,2},{7,3},{8,12},{9,13},{10,... | collective-permute-start | bytes 196616 | tf_op jit(solution)/shard_map/ppermute | solution.py:157
  32.2 3.0 %collective-permute-done.9 = f32[128,128]{1,0:T(8,128)S(1)} collective-permute-done((f32[128,128]{1,0:T(8,128)S(1)}, f32[128,128]{1,0:T(8,128)S(1)}, u32[]{:S(2)}, u32[]{:S(2)}) %collective-permute-start.9) | collective-permute-done | bytes 65568 | tf_op jit(solution)/shard_map/ppermute | solution.py:157
  35.3 0.8 %collective-permute-start.10 = (f32[128,128]{1,0:T(8,128)S(1)}, f32[128,128]{1,0:T(8,128)S(1)}, u32[]{:S(2)}, u32[]{:S(2)}) collective-permute-start(f32[128,128]{1,0:T(8,128)S(1)} %add.44), channel_id=1, source_target_pairs={{0,8},{1,9},{2,10},{3,11},{4,12},{5,13},{6,14},{7,15},{8,0},{9,1},... | collective-permute-start | bytes 196616 | tf_op jit(solution)/shard_map/ppermute | solution.py:157
  36.1 4.4 %collective-permute-done.10 = f32[128,128]{1,0:T(8,128)S(1)} collective-permute-done((f32[128,128]{1,0:T(8,128)S(1)}, f32[128,128]{1,0:T(8,128)S(1)}, u32[]{:S(2)}, u32[]{:S(2)}) %collective-permute-start.10) | collective-permute-done | bytes 65568 | tf_op jit(solution)/shard_map/ppermute | solution.py:157
  40.5 0.6 %add.45 = f32[128,128]{1,0:T(8,128)} add(f32[128,128]{1,0:T(8,128)S(1)} %add.44, f32[128,128]{1,0:T(8,128)S(1)} %collective-permute-done.10) | non-fusion elementwise | flops 16384 | bytes 196608 | tf_op jit(solution)/shard_map/add | solution.py:157
  (3 shorter events, 0.0 us)
Async XLA Ops:
  0.6 9.3 %collective-permute-start.2 = (f32[256,128]{1,0:T(8,128)}, f32[256,128]{1,0:T(8,128)S(1)}, u32[]{:S(2)}, u32[]{:S(2)}) collective-permute-start(f32[256,128]{1,0:T(8,128)} %own_ref.1), channel_id=1, source_target_pairs={{4,0},{5,1},{6,2},{7,3},{8,4},{9,5},{10,6},{11,7},{12,8},{13,9},{1... | collective-permute-start | bytes 393224 | tf_op jit(solution)/shard_map/ppermute | solution.py:100
  5.7 8.1 %collective-permute-start.3 = (f32[256,128]{1,0:T(8,128)}, f32[256,128]{1,0:T(8,128)S(1)}, u32[]{:S(2)}, u32[]{:S(2)}) collective-permute-start(f32[256,128]{1,0:T(8,128)} %own_ref.1), channel_id=1, source_target_pairs={{12,0},{13,1},{14,2},{15,3},{0,4},{1,5},{2,6},{3,7},{4,8},{5,9},{6... | collective-permute-start | bytes 393224 | tf_op jit(solution)/shard_map/ppermute | solution.py:100
  5.7 16.7 %collective-permute-start = (f32[256,128]{1,0:T(8,128)}, f32[256,128]{1,0:T(8,128)S(1)}, u32[]{:S(2)}, u32[]{:S(2)}) collective-permute-start(f32[256,128]{1,0:T(8,128)} %own_ref.1), channel_id=1, source_target_pairs={{1,0},{2,1},{3,2},{4,3},{5,4},{6,5},{7,6},{8,7},{9,8},{10,9},{11,1... | collective-permute-start | bytes 393224 | tf_op jit(solution)/shard_map/ppermute | solution.py:100
  9.4 13.0 %collective-permute-start.1 = (f32[256,128]{1,0:T(8,128)}, f32[256,128]{1,0:T(8,128)S(1)}, u32[]{:S(2)}, u32[]{:S(2)}) collective-permute-start(f32[256,128]{1,0:T(8,128)} %own_ref.1), channel_id=1, source_target_pairs={{15,0},{0,1},{1,2},{2,3},{3,4},{4,5},{5,6},{6,7},{7,8},{8,9},{9,10... | collective-permute-start | bytes 393224 | tf_op jit(solution)/shard_map/ppermute | solution.py:100
  9.4 13.7 %collective-permute-start.4 = (f32[256,128]{1,0:T(8,128)}, f32[256,128]{1,0:T(8,128)S(1)}, u32[]{:S(2)}, u32[]{:S(2)}) collective-permute-start(f32[256,128]{1,0:T(8,128)} %own_ref.1), channel_id=1, source_target_pairs={{8,0},{9,1},{10,2},{11,3},{12,4},{13,5},{14,6},{15,7},{0,8},{1,9},... | collective-permute-start | bytes 393224 | tf_op jit(solution)/shard_map/ppermute | solution.py:100
  10.0 13.2 %collective-permute-start.5 = (f32[256,128]{1,0:T(8,128)S(1)}, f32[256,128]{1,0:T(8,128)S(1)}, u32[]{:S(2)}, u32[]{:S(2)}) collective-permute-start(f32[256,128]{1,0:T(8,128)S(1)} %collective-permute-done.2.refs_2_), channel_id=1, source_target_pairs={{1,0},{2,1},{3,2},{4,3},{5,4},{6,5},{7,6},{8,7},{9,8},{10,9},{11,1... | collective-permute-start | bytes 393224 | tf_op jit(solution)/shard_map/ppermute | solution.py:100
  13.8 9.3 %collective-permute-start.6 = (f32[256,128]{1,0:T(8,128)S(1)}, f32[256,128]{1,0:T(8,128)S(1)}, u32[]{:S(2)}, u32[]{:S(2)}) collective-permute-start(f32[256,128]{1,0:T(8,128)S(1)} %collective-permute-done.3.refs_3_), channel_id=1, source_target_pairs={{15,0},{0,1},{1,2},{2,3},{3,4},{4,5},{5,6},{6,7},{7,8},{8,9},{9,10... | collective-permute-start | bytes 393224 | tf_op jit(solution)/shard_map/ppermute | solution.py:100
  16.0 1.6 %copy-start = (f32[128,4096]{1,0:T(8,128)S(1)}, f32[128,4096]{1,0:T(8,128)}, u32[]{:S(2)}) copy-start(f32[128,4096]{1,0:T(8,128)} %blocks_ref.1) | copy-start | bytes 6291460
  17.6 0.9 %copy-start.1 = (f32[256,128]{1,0:T(8,128)S(1)}, f32[256,128]{1,0:T(8,128)}, u32[]{:S(2)}) copy-start(f32[256,128]{1,0:T(8,128)} %own_ref.1) | copy-start | bytes 393220
  24.3 1.3 %collective-permute-start.7 = (f32[128,128]{1,0:T(8,128)S(1)}, f32[128,128]{1,0:T(8,128)S(1)}, u32[]{:S(2)}, u32[]{:S(2)}) collective-permute-start(f32[128,128]{1,0:T(8,128)S(1)} %get-tuple-element.13), channel_id=1, source_target_pairs={{0,1},{1,0},{2,3},{3,2},{4,5},{5,4},{6,7},{7,6},{8,9},{9,8},{10,11... | collective-permute-start | bytes 196616 | tf_op jit(solution)/shard_map/ppermute | solution.py:157
  25.6 5.3 %collective-permute-start.8 = (f32[128,128]{1,0:T(8,128)S(1)}, f32[128,128]{1,0:T(8,128)S(1)}, u32[]{:S(2)}, u32[]{:S(2)}) collective-permute-start(f32[128,128]{1,0:T(8,128)S(1)} %add.42), channel_id=1, source_target_pairs={{0,2},{1,3},{2,0},{3,1},{4,6},{5,7},{6,4},{7,5},{8,10},{9,11},{10,... | collective-permute-start | bytes 196616 | tf_op jit(solution)/shard_map/ppermute | solution.py:157
  30.9 4.3 %collective-permute-start.9 = (f32[128,128]{1,0:T(8,128)S(1)}, f32[128,128]{1,0:T(8,128)S(1)}, u32[]{:S(2)}, u32[]{:S(2)}) collective-permute-start(f32[128,128]{1,0:T(8,128)S(1)} %add.43), channel_id=1, source_target_pairs={{0,4},{1,5},{2,6},{3,7},{4,0},{5,1},{6,2},{7,3},{8,12},{9,13},{10,... | collective-permute-start | bytes 196616 | tf_op jit(solution)/shard_map/ppermute | solution.py:157
  35.3 5.2 %collective-permute-start.10 = (f32[128,128]{1,0:T(8,128)S(1)}, f32[128,128]{1,0:T(8,128)S(1)}, u32[]{:S(2)}, u32[]{:S(2)}) collective-permute-start(f32[128,128]{1,0:T(8,128)S(1)} %add.44), channel_id=1, source_target_pairs={{0,8},{1,9},{2,10},{3,11},{4,12},{5,13},{6,14},{7,15},{8,0},{9,1},... | collective-permute-start | bytes 196616 | tf_op jit(solution)/shard_map/ppermute | solution.py:157
